TPU v7x, 256 devices: a whole 4x4x8 slice. The times are simulated.
256 devices in a mesh: row: 16 (over z_hi, x), col: 16 (over z_lo, y, core).
Axes of the slice: x: 4, y: 4, z: 8 (z_hi: 4, z_lo: 2; z = z_hi * 2 + z_lo), core: 2. Of those that a mesh axis runs over, the one named last changes fastest.
Arguments:
- features: bfloat16 [131072, 8192], P(('row', 'col')), may hold values from -18 to 18
- prior: float32 [512], replicated, may hold values from 32768 to 524288
Outputs:
- panel_rows: float32 [16, 512, 512], P('row')
- trailing_update: float32 [16, 512, 16, 512], P('row', None, 'col')
All inputs are finite; a program needn't handle non-finite values.
Results may differ from a plain program's by a relative error of at most 0.0054.
Values may be sent and summed in bfloat16 or wider, within the bound.
A program may use at most 128 MiB of HBM per device.

v0:
```python
import jax
import jax.numpy as jnp
from jax import lax
from jax.sharding import PartitionSpec as P

W = 8192
BLOCK = 256
PANEL = 512


def from_root(shard, axis, root):
    mine = lax.axis_index(axis) == root
    return lax.psum(jnp.where(mine, shard, jnp.zeros_like(shard)), axis)


def inverse_factor(tile):
    lower = jnp.linalg.cholesky(tile)
    return jax.scipy.linalg.solve_triangular(
        lower, jnp.eye(tile.shape[0], dtype=jnp.float32), lower=True
    )


def times_t(left, right):
    return jnp.dot(
        left, right.T, precision=lax.Precision.HIGHEST, preferred_element_type=jnp.float32
    )


def select_blocks(gathered, row_count, cycles, col_count, col_cycles, col_rank):
    wanted = lax.iota(jnp.int32, col_cycles) * col_count + col_rank
    picks = wanted % row_count * cycles + wanted // row_count
    return jnp.take(gathered.reshape(row_count * cycles, BLOCK, PANEL), picks, axis=0).reshape(
        col_cycles * BLOCK, PANEL
    )


def on_device(features, prior):
    row_count = lax.axis_size("row")
    col_count = lax.axis_size("col")
    row_rank = lax.axis_index("row")
    col_rank = lax.axis_index("col")
    cycles = W // (BLOCK * row_count)
    col_cycles = W // (BLOCK * col_count)
    partial_value = lax.dot_general(
        features, features[:, :PANEL], (((0,), (0,)), ((), ())), preferred_element_type=jnp.float32
    )
    narrow = PANEL // col_count
    split = partial_value.reshape(cycles, row_count, BLOCK, col_count, narrow).transpose(
        1, 3, 0, 2, 4
    )
    split = split.reshape(row_count * col_count, cycles * BLOCK, narrow)
    mine = lax.psum_scatter(split, ("row", "col"), scatter_dimension=0, tiled=True)[0]
    local = lax.all_gather(mine, "col", axis=1, tiled=True)
    columns = lax.iota(jnp.int32, PANEL)
    offsets = lax.iota(jnp.int32, BLOCK)
    hit = columns[None, :] == offsets[:, None] + row_rank * BLOCK
    local = local.at[:BLOCK].add(
        jnp.where(hit, prior[None, :], jnp.zeros((BLOCK, PANEL), jnp.float32))
    )
    pivot = from_root(local[:BLOCK, :BLOCK], "row", 0)
    inv_first = inverse_factor(pivot)
    first = times_t(local[:, :BLOCK], inv_first)
    lead = from_root(first[:BLOCK], "row", 1)
    rest = local[:, BLOCK:] - times_t(first, lead)
    inv_second = inverse_factor(from_root(rest[:BLOCK], "row", 1))
    second = times_t(rest, inv_second)
    block_ids = lax.iota(jnp.int32, cycles * BLOCK) // BLOCK * row_count + row_rank
    second = jnp.where(block_ids[:, None] >= 1, second, jnp.zeros_like(second))
    panel = jnp.concatenate([first, second], 1)
    rounded = panel.astype(jnp.bfloat16)
    gathered = lax.all_gather(rounded, "row", axis=0, tiled=True)
    chosen = select_blocks(gathered, row_count, cycles, col_count, col_cycles, col_rank)
    update = (
        lax.dot_general(
            rounded, chosen, (((1,), (1,)), ((), ())), preferred_element_type=jnp.float32
        )
        / PANEL
    )
    return (panel[None], update[None, :, None, :])


def solution(mesh):
    placed = (P(("row", "col"), None), P())
    return jax.shard_map(
        on_device,
        mesh=mesh,
        in_specs=placed,
        out_specs=(P("row", None, None), P("row", None, "col", None)),
        check_vma=False,
    )
```

profile of v0, /device:TPU:1, one launch (start us, length us, event | category | flops | bytes accessed | tf_op | source)
XLA Modules:
  0.0 2176.0 jit_solution(13384850917283278144)
XLA Ops:
  7.2 7.1 fusion.6
  14.3 8.8 copy.21
  23.1 24.3 %copy.11 = f32[16,16,2,256,32]{3,2,4,1,0:T(2,128)} copy(f32[16,16,2,256,32]{3,0,2,4,1:T(8,128)} %bitcast.93) | data formatting | bytes 33554432 | tf_op jit(solution)/shard_map/transpose | solution.py:48
  47.4 21.6 reshape.175
  69.1 1292.7 %reduce-scatter.2.cloned.1.call-done = f32[1,512,32]{1,2,0:T(8,128)} async-done(((f32[256,512,32]{1,2,0:T(8,128)}), f32[1,512,32]{1,2,0:T(8,128)}) %reduce-scatter.2.cloned.1.call-update) | async-done | bytes 65552 | tf_op jit(solution)/shard_map/reduce_scatter | solution.py:52
  1361.9 38.1 %all-gather.6.cloned.1.call-done = f32[1,512,512]{1,2,0:T(8,128)} async-done(((f32[1,512,32]{1,2,0:T(8,128)}), f32[1,512,512]{1,2,0:T(8,128)}) %all-gather.6.cloned.1.call-update) | async-done | bytes 1048592 | tf_op jit(solution)/shard_map/all_gather | solution.py:53
  1400.0 1.2 copy.24
  1401.2 1.2 constant_dynamic-update-slice_fusion.4
  1402.4 0.7 slice_select_fusion.2
  1403.4 153.9 %all-reduce.5.cloned.1.call-done = f32[256,256]{0,1:T(8,128)} async-done(((f32[256,256]{0,1:T(8,128)}), f32[256,256]{0,1:T(8,128)}) %all-reduce.5.cloned.1.call-update) | async-done | bytes 262160 | tf_op jit(solution)/shard_map/psum | solution.py:13
  1557.3 1.1 copy.12
  1558.4 1.0 fusion.15
  1559.4 11.7 cholesky.130
  1571.2 9.8 custom-call.13
  1581.4 11.7 cholesky.147
  1593.2 0.7 compare_reduce_fusion.2
  1595.4 4.3 while.5
  1595.6 0.6 fusion.63
  1596.2 1.4 bitcast_dynamic-update-slice_fusion.4
  1597.7 0.6 fusion.63
  1598.3 1.4 bitcast_dynamic-update-slice_fusion.4
  1599.7 19.7 custom-call.14
  1620.3 0.6 fusion.3
  1620.9 0.7 slice_select_fusion.1
  1621.7 163.4 %all-reduce.7.cloned.1.call-done = f32[256,256]{0,1:T(8,128)} async-done(((f32[256,256]{0,1:T(8,128)}), f32[256,256]{0,1:T(8,128)}) %all-reduce.7.cloned.1.call-update) | async-done | bytes 262160 | tf_op jit(solution)/shard_map/psum | solution.py:13
  1785.1 1.6 convolution_subtract_fusion
  1786.8 0.7 slice_select_fusion
  1787.6 164.0 %all-reduce.9.cloned.1.call-done = f32[256,256]{0,1:T(8,128)} async-done(((f32[256,256]{0,1:T(8,128)}), f32[256,256]{0,1:T(8,128)}) %all-reduce.9.cloned.1.call-update) | async-done | bytes 262160 | tf_op jit(solution)/shard_map/psum | solution.py:13
  1951.5 1.1 copy.14
  1952.6 1.0 fusion.14
  1953.6 11.7 cholesky.164
  1965.4 9.8 custom-call.15
  1975.7 11.7 cholesky.181
  1987.4 0.6 compare_reduce_fusion.1
  1988.1 0.7 compare_reduce_fusion
  1990.2 4.4 while.6
  1990.5 0.6 fusion.64
  1991.1 1.4 bitcast_dynamic-update-slice_fusion.5
  1992.5 0.6 fusion.64
  1993.1 1.4 bitcast_dynamic-update-slice_fusion.5
  1994.6 19.7 custom-call.16
  2015.1 0.6 convolution_select_fusion
  2015.8 0.9 fusion.1
  2016.9 1.3 copy.16
  2018.2 131.9 %all-gather.4.cloned.1.call-done = bf16[8192,512]{0,1:T(8,128)(2,1)} async-done(((bf16[512,512]{0,1:T(8,128)(2,1)}), bf16[8192,512]{0,1:T(8,128)(2,1)}) %all-gather.4.cloned.1.call-update) | async-done | bytes 8388624 | tf_op jit(solution)/shard_map/all_gather | solution.py:71
  2150.1 11.9 copy.20
  2162.0 4.0 gather_fusion
  2166.6 2.0 copy.17
  (55 shorter events, 4.5 us)
Async XLA Ops:
  7.2 1354.6 %reduce-scatter.2.cloned.1.call-start = ((), (), s32[]{:S(2)}) async-start(), calls=%async_computation.1 | async-start | bytes 16842752 | tf_op jit(solution)/shard_map/reduce_scatter | solution.py:52
  69.0 1332.2 %copy-start.1 = (f32[512]{0:T(512)S(1)}, f32[512]{0:T(512)}, u32[]{:S(2)}) copy-start(f32[512]{0:T(512)} %param.8) | copy-start | bytes 6148
  69.0 1331.0 %all-gather.6.cloned.1.call-start = ((), (), s32[]{:S(2)}) async-start(), calls=%async_computation.6 | async-start | bytes 1114112 | tf_op jit(solution)/shard_map/all_gather | solution.py:53
  1361.8 195.5 %all-reduce.5.cloned.1.call-start = ((), (), s32[]{:S(2)}) async-start(), calls=%async_computation.2 | async-start | bytes 524288 | tf_op jit(solution)/shard_map/psum | solution.py:13
  1403.1 382.0 %all-reduce.7.cloned.1.call-start = ((), (), s32[]{:S(2)}) async-start(), calls=%async_computation.3 | async-start | bytes 524288 | tf_op jit(solution)/shard_map/psum | solution.py:13
  1621.7 329.8 %all-reduce.9.cloned.1.call-start = ((), (), s32[]{:S(2)}) async-start(), calls=%async_computation.4 | async-start | bytes 524288 | tf_op jit(solution)/shard_map/psum | solution.py:13
  1787.5 362.6 %all-gather.4.cloned.1.call-start = ((), (), s32[]{:S(2)}) async-start(), calls=%async_computation.5 | async-start | bytes 8912896 | tf_op jit(solution)/shard_map/all_gather | solution.py:71
  2018.2 147.9 %copy-start = (bf16[512,512]{0,1:T(8,128)(2,1)S(1)}, bf16[512,512]{0,1:T(8,128)(2,1)}, u32[]{:S(2)}) copy-start(bf16[512,512]{0,1:T(8,128)(2,1)} %fusion.1) | copy-start | bytes 1572868
Sparse Core Ops, SparseCore 0:
  69.1 1292.6 reduce-scatter.1
  1363.8 36.1 all-gather.5
  1403.4 153.8 all-reduce.4
  1621.8 163.2 all-reduce.6
  1788.3 163.1 all-reduce.8
  2016.8 133.2 all-gather.3
where the time goes:
time: 2190 us; the launch traced here: 2180 us
  waiting for transfers between devices  1940 us (89%)
  other arithmetic  115 us (5%)
  local copies, waits for them, and re-layouts  85.6 us (4%)
    reduce_scatter x1, waiting for transfers between devices, on_device(): lax.psum_scatter(split, ('row', 'col'), scatter_dimension=0, tiled=True)[0]  1290 us
    psum x3, waiting for transfers between devices, from_root(): return lax.psum(jnp.where(mine, shard, jnp.zeros_like(shard)), axis)  481 us
    all_gather x1, waiting for transfers between devices, on_device(): gathered = lax.all_gather(rounded, 'row', axis=0, tiled=True)  132 us
    another operation x13, other arithmetic, inverse_factor(): lower = jnp.linalg.cholesky(tile)  68.7 us
  transfers between devices with their start and end apart: 6, of which 6 were waited for; matrix products, arithmetic and copies ran while one was open for 0% of the time, Pallas kernels for 0%

commit v1 on v0

v1 whole, which is shorter than its diff:
```python
import jax
import jax.numpy as jnp
from jax import lax
from jax.experimental import pallas as pl
from jax.experimental.pallas import tpu as pltpu
from jax.sharding import PartitionSpec as P

W = 8192
BLOCK = 256
PANEL = 512
TOKENS = 512
HALF = W // 2
MESH = pl.DeviceIdType.MESH
WIRE = jnp.bfloat16
F32 = jnp.float32
ORDERS = (
    ("xa", "xb", "ya", "yb"),
    ("xb", "ya", "yb", "xa"),
    ("ya", "yb", "xa", "xb"),
    ("yb", "xa", "xb", "ya"),
)
FULL = slice(None)


class Place:
    def __init__(self):
        self.r = lax.axis_index("row")
        self.c = lax.axis_index("col")
        self.x = self.r % 4
        self.y = (self.c // 2) % 4
        self.zh = self.r // 4
        self.zl = self.c // 8
        self.z = self.zh * 2 + self.zl
        self.core = self.c % 2
        self.bits = {
            "xa": ((self.x + 1) // 2) % 2,
            "xb": self.x // 2,
            "ya": ((self.y + 1) // 2) % 2,
            "yb": self.y // 2,
        }

    def at(self, x=None, y=None, z=None, core=None):
        x = self.x if x is None else x
        y = self.y if y is None else y
        z = self.z if z is None else z
        core = self.core if core is None else core
        return (z // 2 * 4 + x, z % 2 * 8 + y * 2 + core)

    def partner(self, dim):
        if dim == "xa":
            return self.at(x=self.x + 1 - 2 * (self.x % 2))
        if dim == "xb":
            return self.at(x=3 - self.x)
        if dim == "ya":
            return self.at(y=self.y + 1 - 2 * (self.y % 2))
        return self.at(y=3 - self.y)


def tile_index(place, quarter, zh, step, last):
    fixed = {}
    for k, dim in enumerate(ORDERS[quarter][: step + 1]):
        mine = place.bits[dim]
        fixed[dim] = mine if (k < step or last) else 1 - mine
    pick = lambda dim: fixed.get(dim, FULL)
    return (zh, pick("xb"), pick("xa"), quarter, pick("ya"), pick("yb"))


def top_index(place, quarter, step, last):
    _, xb, xa, _, ya, yb = tile_index(place, quarter, 0, step, last)
    return (quarter, ya, yb, xb, xa)


def gather_kernel(feat, rows_out, top_out, own, theirs, lead_own, lead_their, lead_t, acc, top,
                  s0, s1, s2, s3, r0, r1, r2, r3, ts0, ts1, ts2, ts3, tr0, tr1, tr2, tr3,
                  zsend, zrecv, zown, topz,
                  load_sem, feat_send, feat_recv, step_send, step_recv, top_send, top_recv,
                  z_send, z_recv, tz_send, tz_recv, tg_send, tg_recv, core_send, core_recv,
                  row_send, row_recv, col_send, col_recv):
    me = Place()
    sends, recvs = (s0, s1, s2, s3), (r0, r1, r2, r3)
    tsends, trecvs = (ts0, ts1, ts2, ts3), (tr0, tr1, tr2, tr3)
    mate = me.at(core=1 - me.core)
    loads = [pltpu.make_async_copy(feat.at[:, pl.ds(0, PANEL)], lead_own, load_sem.at[0])]
    for i in range(4):
        loads.append(
            pltpu.make_async_copy(
                feat.at[:, pl.ds(pl.multiple_of(me.core * HALF + i * 1024, 1024), 1024)],
                own.at[:, pl.ds(i * 1024, 1024)],
                load_sem.at[i + 1],
            )
        )
    for load in loads:
        load.start()

    barrier = pltpu.get_barrier_semaphore()

    def greet(device):
        pl.semaphore_signal(barrier, inc=1, device_id=device, device_id_type=MESH)

    greet(mate)
    for dim in ORDERS[0]:
        greet(me.partner(dim))
    for j in range(1, 8):
        greet(me.at(z=(me.z + j) % 8))
    pl.semaphore_wait(barrier, 12)

    shares = [
        pltpu.make_async_remote_copy(
            src_ref=feat.at[:, pl.ds(0, PANEL)], dst_ref=lead_their,
            send_sem=feat_send.at[0], recv_sem=feat_recv.at[0],
            device_id=mate, device_id_type=MESH,
        )
    ]
    for i in range(4):
        shares.append(
            pltpu.make_async_remote_copy(
                src_ref=feat.at[:, pl.ds(pl.multiple_of((1 - me.core) * HALF + i * 1024, 1024), 1024)],
                dst_ref=theirs.at[:, pl.ds(i * 1024, 1024)],
                send_sem=feat_send.at[i + 1], recv_sem=feat_recv.at[i + 1],
                device_id=mate, device_id_type=MESH,
            )
        )
    for share in shares:
        share.start()

    loads[0].wait()
    lead_t[:, :TOKENS] = lead_own[...].T
    shares[0].wait_recv()
    lead_t[:, TOKENS:] = lead_their[...].T

    def products(left, right):
        return jnp.dot(lead_t[:, :TOKENS], left, preferred_element_type=F32) + jnp.dot(
            lead_t[:, TOKENS:], right, preferred_element_type=F32
        )

    lanes = pl.ds(pl.multiple_of(me.core * BLOCK, BLOCK), BLOCK)
    top[...] = products(lead_own[:, lanes], lead_their[:, lanes]).reshape(4, 2, 2, 2, 2, 8, BLOCK)

    def exchange(src, dst, send, recv, device):
        return pltpu.make_async_remote_copy(
            src_ref=src, dst_ref=dst, send_sem=send, recv_sem=recv,
            device_id=device, device_id_type=MESH,
        )

    def top_copy(step, q):
        return exchange(
            tsends[step].at[q], trecvs[step].at[q], top_send.at[step, q], top_recv.at[step, q],
            me.partner(ORDERS[q][step]),
        )

    def top_start(step):
        for q in range(4):
            tsends[step][q] = top[top_index(me, q, step, False)]
            top_copy(step, q).start()

    def top_finish(step):
        for q in range(4):
            top_copy(step, q).wait_recv()
            at = top_index(me, q, step, True)
            top[at] = top[at] + trecvs[step][q]

    def main_copy(step, zh, q):
        return exchange(
            sends[step].at[zh, q], recvs[step].at[zh, q],
            step_send.at[step, zh, q], step_recv.at[step, zh, q],
            me.partner(ORDERS[q][step]),
        )

    def main_start(step, zh):
        for q in range(4):
            sends[step][zh, q] = acc[tile_index(me, q, zh, step, False)].astype(WIRE)
            main_copy(step, zh, q).start()

    def main_finish(step, zh):
        for q in range(4):
            main_copy(step, zh, q).wait_recv()
            at = tile_index(me, q, zh, step, True)
            acc[at] = acc[at] + recvs[step][zh, q].astype(F32)

    def multiply(zh):
        loads[zh + 1].wait()
        shares[zh + 1].wait_recv()

        def body(p, carry):
            xb, xa = p // 2, p % 2
            x = 2 * xb + (xb + xa) % 2
            at = pl.ds(pl.multiple_of((zh * 4 + x) * BLOCK, BLOCK), BLOCK)
            acc[zh, xb, xa] = products(own[:, at], theirs[:, at]).reshape(4, 2, 2, 32, BLOCK)
            return carry

        lax.fori_loop(0, 4, body, 0)

    my_top = (me.bits["ya"], me.bits["yb"], me.bits["xb"], me.bits["xa"])
    my_slot = 8 * my_top[0] + 4 * my_top[1] + 2 * my_top[2] + my_top[3]
    top_start(0)
    for wave in range(8):
        if wave >= 1 and wave <= 4:
            top_finish(wave - 1)
            if wave < 4:
                top_start(wave)
            else:
                for q in range(4):
                    topz[me.z, q] = top[(q,) + my_top]
                top_plane = [
                    exchange(topz.at[me.z], topz.at[me.z], tz_send.at[j - 1], tz_recv,
                             me.at(z=(me.z + j) % 8))
                    for j in range(1, 8)
                ]
                for copy in top_plane:
                    copy.start()
        if wave < 4:
            multiply(wave)
            main_start(0, wave)
        if wave == 5:
            pltpu.make_async_copy(topz.at[pl.ds(0, 7)], topz.at[pl.ds(0, 7)], tz_recv).wait()
            for q in range(4):
                total = topz[0, q]
                for z in range(1, 8):
                    total = total + topz[z, q]
                top_out[me.core, my_slot, q] = total
            top_gather = [
                exchange(top_out.at[me.core, my_slot], top_out.at[me.core, my_slot],
                         tg_send.at[j - 1], tg_recv,
                         me.at(x=(me.x + j) % 4, y=(me.y + j // 4) % 4))
                for j in range(1, 16)
            ]
            for copy in top_gather:
                copy.start()
        for step in range(4):
            zh = wave - step - 1
            if 0 <= zh < 4:
                main_finish(step, zh)
                if step < 3:
                    main_start(step + 1, zh)
        if wave == 6:
            fifteen = top_out.at[me.core, pl.ds(0, 15)]
            pltpu.make_async_copy(fifteen, fifteen, tg_recv).wait()
            top_mate = exchange(top_out.at[me.core], top_out.at[me.core], core_send, core_recv, mate)
            top_mate.start()

    home = lambda q, zh: (zh, me.bits["xb"], me.bits["xa"], q, me.bits["ya"], me.bits["yb"])
    for q in range(4):
        for zh in range(4):
            tile = acc[home(q, zh)]
            for zl in range(2):
                zsend[zh * 2 + zl, q] = tile[:, zl * 128 : zl * 128 + 128].astype(WIRE)
        tile = acc[home(q, me.zh)]
        for zl in range(2):
            zown[zl, q] = tile[:, zl * 128 : zl * 128 + 128]
    plane = [
        exchange(zsend.at[(me.z + j) % 8], zrecv.at[me.z], z_send.at[j - 1], z_recv,
                 me.at(z=(me.z + j) % 8))
        for j in range(1, 8)
    ]
    for copy in plane:
        copy.start()
    pltpu.make_async_copy(zrecv.at[pl.ds(0, 7)], zrecv.at[pl.ds(0, 7)], z_recv).wait()
    slot = 8 * me.core + 4 * me.zl + 2 * me.bits["ya"] + me.bits["yb"]
    for q in range(4):
        total = zown[me.zl, q]
        for j in range(1, 8):
            total = total + zrecv[(me.z + j) % 8, q].astype(F32)
        rows_out[0, slot, q] = total.astype(rows_out.dtype)
    mine = rows_out.at[0, slot]
    row_copies = [
        exchange(mine, mine, row_send.at[j - 1], row_recv, (me.r, (me.c + j) % 16))
        for j in range(1, 16)
    ]
    col_copies = [
        exchange(mine, rows_out.at[1, slot], col_send.at[j], col_recv, ((me.r + j) % 16, me.r))
        for j in range(16)
    ]
    for j in range(1, 16):
        col_copies[j].start()
        row_copies[j - 1].start()

    @pl.when(me.r != me.c)
    def _():
        col_copies[0].start()

    @pl.when(me.r == me.c)
    def _():
        rows_out[1, slot] = rows_out[0, slot]

    top_mate.wait()
    fifteen = rows_out.at[0, pl.ds(0, 15)]
    pltpu.make_async_copy(fifteen, fifteen, row_recv).wait()

    @pl.when(me.r != me.c)
    def _():
        pltpu.make_async_copy(rows_out.at[1], rows_out.at[1], col_recv).wait()
        col_copies[0].wait_send()

    @pl.when(me.r == me.c)
    def _():
        pltpu.make_async_copy(fifteen, fifteen, col_recv).wait()

    for copies in (row_copies, col_copies[1:], plane, top_plane, top_gather, shares):
        for copy in copies:
            copy.wait_send()
    for step in range(4):
        for q in range(4):
            top_copy(step, q).wait_send()
            for zh in range(4):
                main_copy(step, zh, q).wait_send()


def gather_rows(features):
    twos = lambda n: (2,) * n
    wire = lambda n: pltpu.VMEM((4, 4) + twos(n) + (32, BLOCK), WIRE)
    exact = lambda n: pltpu.VMEM((4,) + twos(n) + (8, BLOCK), F32)
    dma = pltpu.SemaphoreType.DMA
    return pl.pallas_call(
        gather_kernel,
        out_shape=(
            jax.ShapeDtypeStruct((2, 16, 4, 32, 128), WIRE),
            jax.ShapeDtypeStruct((2, 16, 4, 8, BLOCK), F32),
        ),
        in_specs=[pl.BlockSpec(memory_space=pl.ANY)],
        out_specs=(pl.BlockSpec(memory_space=pltpu.VMEM),) * 2,
        scratch_shapes=[
            pltpu.VMEM((TOKENS, HALF), jnp.bfloat16),
            pltpu.VMEM((TOKENS, HALF), jnp.bfloat16),
            pltpu.VMEM((TOKENS, PANEL), jnp.bfloat16),
            pltpu.VMEM((TOKENS, PANEL), jnp.bfloat16),
            pltpu.VMEM((PANEL, 2 * TOKENS), jnp.bfloat16),
            pltpu.VMEM((4, 2, 2, 4, 2, 2, 32, BLOCK), F32),
            pltpu.VMEM((4, 2, 2, 2, 2, 8, BLOCK), F32),
            *[wire(n) for n in (3, 2, 1, 0)],
            *[wire(n) for n in (3, 2, 1, 0)],
            *[exact(n) for n in (3, 2, 1, 0)],
            *[exact(n) for n in (3, 2, 1, 0)],
            pltpu.VMEM((8, 4, 32, 128), WIRE),
            pltpu.VMEM((8, 4, 32, 128), WIRE),
            pltpu.VMEM((2, 4, 32, 128), F32),
            pltpu.VMEM((8, 4, 8, BLOCK), F32),
            dma((5,)), dma((5,)), dma((5,)),
            dma((4, 4, 4)), dma((4, 4, 4)), dma((4, 4)), dma((4, 4)),
            dma((7,)), dma, dma((7,)), dma, dma((15,)), dma, dma, dma,
            dma((15,)), dma, dma((16,)), dma,
        ],
        compiler_params=pltpu.CompilerParams(
            collective_id=1, has_side_effects=True, vmem_limit_bytes=56 * 2**20
        ),
        cost_estimate=pl.CostEstimate(
            flops=2 * PANEL * 1024 * HALF, bytes_accessed=10 * 2**20, transcendentals=0
        ),
        name="reduce_gram",
    )(features)


def inverse_factor(tile):
    lower = jnp.linalg.cholesky(tile)
    return jax.scipy.linalg.solve_triangular(
        lower, jnp.eye(tile.shape[0], dtype=jnp.float32), lower=True
    )


def dot(left, right):
    return jnp.dot(left, right, precision=lax.Precision.HIGHEST, preferred_element_type=F32)


def on_device(features, prior):
    r, c = lax.axis_index("row"), lax.axis_index("col")
    rows, top = gather_rows(features)
    top = top.transpose(2, 1, 3, 0, 4).reshape(PANEL, PANEL) + jnp.diag(prior)
    gram = rows.astype(F32).reshape(2, 2, 2, 4, 4, 32, 128).transpose(0, 4, 3, 5, 1, 2, 6).reshape(2, PANEL, PANEL)
    own = jnp.stack([r, c])
    exact = jnp.where((own == 0)[:, None, None], top[None, :, :BLOCK], top[None, :, BLOCK:])
    gram = gram.at[:, :, :BLOCK].set(
        jnp.where((own < 2)[:, None, None], exact, gram[:, :, :BLOCK])
    )
    gram = gram.transpose(1, 0, 2).reshape(PANEL, 2 * PANEL)
    inv_first = inverse_factor(top[:BLOCK, :BLOCK])
    lead = dot(top[BLOCK:, :BLOCK], inv_first.T)
    inv_second = inverse_factor(top[BLOCK:, BLOCK:] - dot(lead, lead.T))
    first = dot(inv_first, gram[:BLOCK])
    second = dot(inv_second, gram[BLOCK:] - dot(lead, first))
    second = second.reshape(BLOCK, 2, PANEL)
    dead = (own == 0)[None, :, None] & (lax.iota(jnp.int32, PANEL) < BLOCK)[None, None, :]
    second = jnp.where(dead, 0.0, second)
    panel = jnp.concatenate([first.reshape(BLOCK, 2, PANEL), second], 0)
    rounded = panel.astype(jnp.bfloat16)
    update = (
        lax.dot_general(
            rounded[:, 0], rounded[:, 1], (((0,), (0,)), ((), ())), preferred_element_type=F32
        )
        / PANEL
    )
    return (panel[:, 0].T[None], update[None, :, None, :])


def solution(mesh):
    placed = (P(("row", "col"), None), P())
    return jax.shard_map(
        on_device,
        mesh=mesh,
        in_specs=placed,
        out_specs=(P("row", None, None), P("row", None, "col", None)),
        check_vma=False,
    )
```

time: 2190 us -> 232 us (0.11)
  the two profiles are of different devices: /device:TPU:1 before, /device:TPU:57 now
where the time goes in v1:
time: 232 us; the launch traced here: 228 us
  other arithmetic  110 us (47%)
  Pallas kernels  79.2 us (34%)
  local copies, waits for them, and re-layouts  23.6 us (10%)
  matrix products  11.2 us (5%)
  between operations  3.85 us (2%)
    pallas_call x1, Pallas kernels, gather_rows(): pl.pallas_call(gather_kernel, out_shape=(jax.ShapeDtypeStruct((2, 16, 4,...  79.2 us
    another operation x13, other arithmetic, inverse_factor(): lower = jnp.linalg.cholesky(tile)  68.8 us
    another operation x5, other arithmetic, inverse_factor(): jax.scipy.linalg.solve_triangular(lower, jnp.eye(tile.shape[0], dtype=jnp...  39.6 us
    another operation x15, local copies, waits for them, and re-layouts, inverse_factor(): jax.scipy.linalg.solve_triangular(lower, jnp.eye(tile.shape[0], dtype=jnp...  8.13 us
    dot_general x4, matrix products, dot(): jnp.dot(left, right, precision=lax.Precision.HIGHEST, preferred_element_t...  5.67 us
    reshape x2, local copies, waits for them, and re-layouts, on_device(): rows.astype(F32).reshape(2, 2, 2, 4, 4, 32, 128)  5.36 us

profile of v1, /device:TPU:57, one launch (start us, length us, event | category | flops | bytes accessed | tf_op | source)
XLA Modules:
  0.0 228.4 jit_solution(14666108241384988624)
XLA Ops:
  0.6 79.2 %reduce_gram.1 = (bf16[2,16,4,32,128]{4,3,2,1,0:T(8,128)(2,1)}, f32[2,16,4,8,256]{4,3,2,1,0:T(8,128)}) custom-call(bf16[512,8192]{1,0:T(8,128)(2,1)} %feat.1), custom_call_target="tpu_custom_call" | custom-call | flops 4294967296 | bytes 10485760 | tf_op jit(solution)/shard_map/reduce_gram/pallas_call | solution.py:313
  79.8 2.0 copy.13
  82.0 0.3 copy.14
  82.9 11.7 %cholesky.130 = f32[128,128]{1,0:T(8,128)S(1)} custom-call(f32[128,128]{1,0:T(8,128)S(1)} %cholesky.194), custom_call_target="Cholesky" | custom-call | tf_op jit(solution)/shard_map/jit(cholesky)/cholesky | solution.py:353
  94.6 9.8 %custom-call.13 = f32[1,128,128]{1,2,0:T(8,128)S(1)} custom-call(f32[1,128,128]{2,1,0:T(8,128)S(1)} %get-tuple-element.71), custom_call_target="InvertDiagBlocksLowerTriangular" | custom-call | tf_op jit(solution)/shard_map/jit(cholesky)/cholesky | solution.py:353
  104.7 0.3 convolution_subtract_fusion.5
  105.0 11.9 %cholesky.147 = f32[128,128]{1,0:T(8,128)S(1)} custom-call(f32[128,128]{1,0:T(8,128)S(1)} %convolution_subtract_fusion.5), custom_call_target="Cholesky" | custom-call | tf_op jit(solution)/shard_map/jit(cholesky)/cholesky | solution.py:353
  116.9 0.6 compare_reduce_fusion.2
  118.9 4.1 %while.5 = (s32[]{:T(128)}, f32[256,256]{1,0:T(8,128)S(1)}, s32[2,2]{1,0:T(2,128)S(1)}, f32[2,128,128]{2,1,0:T(8,128)S(1)}, s32[]{:T(128)}) while((s32[]{:T(128)}, f32[256,256]{1,0:T(8,128)S(1)}, s32[2,2]{1,0:T(2,128)S(1)}, f32[2,128,128]{2,1,0:T(8,128)S(1)}, s32[]{:T(128)}) %tuple.56), condition=%wide.while_cond.1, body=%wide.while_body.1.sunk | while | flops 2 | bytes 131181 | solution.py:354
  119.0 0.7 fusion.52
  119.6 1.3 bitcast_dynamic-update-slice_fusion.4
  121.0 0.7 fusion.52
  121.7 1.3 bitcast_dynamic-update-slice_fusion.4
  123.0 19.7 %custom-call.14 = f32[2,128,128]{1,2,0:T(8,128)S(1)} custom-call(f32[2,128,128]{2,1,0:T(8,128)S(1)} %get-tuple-element.34), custom_call_target="InvertDiagBlocksLowerTriangular" | custom-call | tf_op jit(solution)/shard_map/jit(_solve_triangular)/triangular_solve | solution.py:354
  142.7 0.3 fusion.17
  143.0 0.3 convolution_subtract_fusion.3
  143.3 1.0 fusion.24
  144.3 1.5 fusion.5
  145.8 0.4 convolution_subtract_fusion.1
  146.4 11.7 %cholesky.164 = f32[128,128]{1,0:T(8,128)S(1)} custom-call(f32[128,128]{1,0:T(8,128)S(1)} %cholesky.197), custom_call_target="Cholesky" | custom-call | tf_op jit(solution)/shard_map/jit(cholesky)/cholesky | solution.py:353
  158.2 9.8 %custom-call.15 = f32[1,128,128]{1,2,0:T(8,128)S(1)} custom-call(f32[1,128,128]{2,1,0:T(8,128)S(1)} %get-tuple-element.67), custom_call_target="InvertDiagBlocksLowerTriangular" | custom-call | tf_op jit(solution)/shard_map/jit(cholesky)/cholesky | solution.py:353
  168.2 0.3 convolution_subtract_fusion.4
  168.5 11.7 %cholesky.181 = f32[128,128]{1,0:T(8,128)S(1)} custom-call(f32[128,128]{1,0:T(8,128)S(1)} %convolution_subtract_fusion.4), custom_call_target="Cholesky" | custom-call | tf_op jit(solution)/shard_map/jit(cholesky)/cholesky | solution.py:353
  180.2 0.6 compare_reduce_fusion
  180.9 0.7 compare_reduce_fusion.1
  182.9 4.1 %while.6 = (s32[]{:T(128)}, f32[256,256]{1,0:T(8,128)S(1)}, s32[2,2]{1,0:T(2,128)S(1)}, f32[2,128,128]{2,1,0:T(8,128)S(1)}, s32[]{:T(128)}) while((s32[]{:T(128)}, f32[256,256]{1,0:T(8,128)S(1)}, s32[2,2]{1,0:T(2,128)S(1)}, f32[2,128,128]{2,1,0:T(8,128)S(1)}, s32[]{:T(128)}) %tuple.62), condition=%wide.while_cond.1.clone, body=%wide.while_body.1.clone.sunk | while | flops 2 | bytes 131181 | solution.py:354
  182.9 0.7 fusion.53
  183.6 1.3 bitcast_dynamic-update-slice_fusion.5
  184.9 0.7 fusion.53
  185.6 1.3 bitcast_dynamic-update-slice_fusion.5
  187.0 19.9 %custom-call.16 = f32[2,128,128]{1,2,0:T(8,128)S(1)} custom-call(f32[2,128,128]{2,1,0:T(8,128)S(1)} %get-tuple-element.35), custom_call_target="InvertDiagBlocksLowerTriangular" | custom-call | tf_op jit(solution)/shard_map/jit(_solve_triangular)/triangular_solve | solution.py:354
  206.9 0.3 fusion.15
  207.5 0.4 copy-done
  207.8 1.0 fusion.20
  209.4 0.7 copy-done.2
  210.1 2.4 %copy.31 = f32[2,2,2,4,4,32,128]{6,2,1,5,3,4,0:T(2,128)} copy(bf16[2,2,2,4,4,32,128]{6,5,4,3,2,1,0:T(8,128)(2,1)S(1)} %bitcast.107) | data formatting | bytes 3145728 | tf_op jit(solution)/shard_map/reshape | solution.py:367
  212.5 2.9 %reshape.192 = f32[2,512,512]{2,1,0:T(8,128)S(1)} reshape(f32[2,4,4,32,2,2,128]{6,5,4,3,2,1,0:T(2,128)} %bitcast.101) | data formatting | bytes 4194304 | tf_op jit(solution)/shard_map/reshape | solution.py:367
  215.5 0.3 fusion.4
  215.8 1.2 fusion.34
  217.0 1.6 copy.19
  218.5 1.9 fusion.14
  220.5 0.3 copy.22
  220.9 1.8 convolution_subtract_fusion
  222.7 1.0 fusion.7
  224.0 0.3 copy.27
  224.5 0.5 fusion.1
  225.0 2.0 copy.25
  227.0 1.1 fusion.3
  (45 shorter events, 2.8 us)
Async XLA Ops:
  81.9 0.7 copy-start.4
  207.2 0.6 copy-start
  208.9 1.2 copy-start.2
  220.8 1.8 copy-start.1
  220.9 1.8 copy-start.3

commit v2 on v1

--- a/solution.py
+++ b/solution.py
@@ -349,45 +349,154 @@
     )(features)
 
 
-def inverse_factor(tile):
-    lower = jnp.linalg.cholesky(tile)
-    return jax.scipy.linalg.solve_triangular(
-        lower, jnp.eye(tile.shape[0], dtype=jnp.float32), lower=True
-    )
+def lane(tile, k):
+    return jnp.broadcast_to(tile[:, k : k + 1], (8, 128))
+
+
+def sublane(tile, k):
+    return jnp.broadcast_to(tile[k : k + 1, :], (8, 128))
+
+
+def pair_sum(terms):
+    while len(terms) > 1:
+        terms = [terms[2 * i] + terms[2 * i + 1] for i in range(len(terms) // 2)]
+    return terms[0]
+
+
+def inverse_128(tile):
+    s = [tile[8 * i : 8 * i + 8] for i in range(16)]
+    rows = lax.broadcasted_iota(jnp.int32, (8, 128), 0)
+    cols = lax.broadcasted_iota(jnp.int32, (8, 128), 1)
+    v = [jnp.where(cols == rows + 8 * i, 1.0, 0.0).astype(F32) for i in range(16)]
+    out = []
+
+    def collect(parts):
+        whole = parts[7]
+        for k in range(6, -1, -1):
+            whole = jnp.where(rows == k, parts[k], whole)
+        return whole
+
+    for p in range(16):
+        near = list(range(p, min(16, p + 2)))
+        m = [[lane(s[g], 8 * p + k) for k in range(8)] for g in near]
+        us, vs = [], []
+        for k in range(8):
+            inv = lax.rsqrt(sublane(m[0][k], k))
+            u, w = sublane(s[p], k) * inv, sublane(v[p], k) * inv
+            us.append(u)
+            vs.append(w)
+            scaled = [sublane(m[0][i], k) * inv for i in range(k + 1, 8)]
+            for n, g in enumerate(near):
+                if n == 0 and k == 7:
+                    continue
+                factor = m[n][k] * inv
+                for i in range(k + 1, 8):
+                    m[n][i] = m[n][i] - factor * scaled[i - k - 1]
+                s[g] = s[g] - factor * u
+                v[g] = v[g] - factor * w
+        out.append(collect(vs))
+        if p + 2 < 16:
+            turned = collect(us).T
+            for i in range(p + 2, 16):
+                group = turned[8 * i : 8 * i + 8]
+                factors = [lane(group, k) for k in range(8)]
+                s[i] = s[i] - pair_sum([f * u for f, u in zip(factors, us)])
+                v[i] = v[i] - pair_sum([f * w for f, w in zip(factors, vs)])
+    return jnp.concatenate(out, 0)
 
 
 def dot(left, right):
     return jnp.dot(left, right, precision=lax.Precision.HIGHEST, preferred_element_type=F32)
 
 
+def dot_t(left, right):
+    return lax.dot_general(
+        left, right, (((1,), (1,)), ((), ())),
+        precision=lax.Precision.HIGHEST, preferred_element_type=F32,
+    )
+
+
+def inverse_256(ref, start, out):
+    lo, hi = pl.ds(start, 128), pl.ds(start + 128, 128)
+    v1 = inverse_128(ref[lo, lo])
+    below = dot_t(ref[hi, lo], v1)
+    v2 = inverse_128(ref[hi, hi] - dot_t(below, below))
+    out[:128, :128] = v1
+    out[:128, 128:] = jnp.zeros((128, 128), F32)
+    out[128:, :128] = -dot(v2, dot(below, v1))
+    out[128:, 128:] = v2
+
+
+def panel_kernel(rows, top, prior, panel_out, update_out, a, g, inv1, inv2, other):
+    r, c = lax.axis_index("row"), lax.axis_index("col")
+    for h in range(2):
+        for q in range(4):
+            for s in range(16):
+                a[pl.ds(128 * q + 8 * s, 8), pl.ds(BLOCK * h, BLOCK)] = top[h, s, q]
+    for b in range(4):
+        at = pl.ds(128 * b, 128)
+        i = lax.broadcasted_iota(jnp.int32, (128, 128), 0)
+        j = lax.broadcasted_iota(jnp.int32, (128, 128), 1)
+        a[at, at] = a[at, at] + jnp.where(i == j, prior[:, at], 0.0)
+    for side in range(2):
+        for h in range(2):
+            for zl in range(2):
+                for s in range(4):
+                    for q in range(4):
+                        g[side, pl.ds(128 * q + 32 * s, 32), pl.ds(BLOCK * h + 128 * zl, 128)] = rows[
+                            side, 8 * h + 4 * zl + s, q
+                        ].astype(F32)
+        own = (r, c)[side]
+        for b in range(2):
+
+            @pl.when(own == b)
+            def _():
+                g[side, :, :BLOCK] = a[:, pl.ds(BLOCK * b, BLOCK)]
+
+    inverse_256(a, 0, inv1)
+    lead = dot_t(a[BLOCK:, :BLOCK], inv1[...])
+    a[BLOCK:, BLOCK:] = a[BLOCK:, BLOCK:] - dot_t(lead, lead)
+    inverse_256(a, BLOCK, inv2)
+
+    for b in range(2):
+        at = pl.ds(BLOCK * b, BLOCK)
+        first = dot_t(g[0, :BLOCK, at].T, inv1[...])
+        second = dot_t(g[0, BLOCK:, at].T - dot_t(first, lead), inv2[...])
+        if b == 0:
+            second = jnp.where(r == 0, 0.0, second)
+        panel_out[0, at, :BLOCK] = first
+        panel_out[0, at, BLOCK:] = second
+    first = dot(inv1[...], g[1, :BLOCK])
+    second = dot(inv2[...], g[1, BLOCK:] - dot(lead, first))
+    other[:BLOCK] = first.astype(jnp.bfloat16)
+    other[BLOCK:, :BLOCK] = jnp.where(c == 0, 0.0, second[:, :BLOCK]).astype(jnp.bfloat16)
+    other[BLOCK:, BLOCK:] = second[:, BLOCK:].astype(jnp.bfloat16)
+    update_out[0] = jnp.dot(
+        panel_out[0].astype(jnp.bfloat16), other[...], preferred_element_type=F32
+    ) * (1.0 / PANEL)
+
+
 def on_device(features, prior):
-    r, c = lax.axis_index("row"), lax.axis_index("col")
     rows, top = gather_rows(features)
-    top = top.transpose(2, 1, 3, 0, 4).reshape(PANEL, PANEL) + jnp.diag(prior)
-    gram = rows.astype(F32).reshape(2, 2, 2, 4, 4, 32, 128).transpose(0, 4, 3, 5, 1, 2, 6).reshape(2, PANEL, PANEL)
-    own = jnp.stack([r, c])
-    exact = jnp.where((own == 0)[:, None, None], top[None, :, :BLOCK], top[None, :, BLOCK:])
-    gram = gram.at[:, :, :BLOCK].set(
-        jnp.where((own < 2)[:, None, None], exact, gram[:, :, :BLOCK])
-    )
-    gram = gram.transpose(1, 0, 2).reshape(PANEL, 2 * PANEL)
-    inv_first = inverse_factor(top[:BLOCK, :BLOCK])
-    lead = dot(top[BLOCK:, :BLOCK], inv_first.T)
-    inv_second = inverse_factor(top[BLOCK:, BLOCK:] - dot(lead, lead.T))
-    first = dot(inv_first, gram[:BLOCK])
-    second = dot(inv_second, gram[BLOCK:] - dot(lead, first))
-    second = second.reshape(BLOCK, 2, PANEL)
-    dead = (own == 0)[None, :, None] & (lax.iota(jnp.int32, PANEL) < BLOCK)[None, None, :]
-    second = jnp.where(dead, 0.0, second)
-    panel = jnp.concatenate([first.reshape(BLOCK, 2, PANEL), second], 0)
-    rounded = panel.astype(jnp.bfloat16)
-    update = (
-        lax.dot_general(
-            rounded[:, 0], rounded[:, 1], (((0,), (0,)), ((), ())), preferred_element_type=F32
-        )
-        / PANEL
-    )
-    return (panel[:, 0].T[None], update[None, :, None, :])
+    panel, update = pl.pallas_call(
+        panel_kernel,
+        out_shape=(
+            jax.ShapeDtypeStruct((1, PANEL, PANEL), F32),
+            jax.ShapeDtypeStruct((1, PANEL, PANEL), F32),
+        ),
+        in_specs=[pl.BlockSpec(memory_space=pltpu.VMEM)] * 3,
+        out_specs=(pl.BlockSpec(memory_space=pltpu.VMEM),) * 2,
+        scratch_shapes=[
+            pltpu.VMEM((PANEL, PANEL), F32),
+            pltpu.VMEM((2, PANEL, PANEL), F32),
+            pltpu.VMEM((BLOCK, BLOCK), F32),
+            pltpu.VMEM((BLOCK, BLOCK), F32),
+            pltpu.VMEM((PANEL, PANEL), jnp.bfloat16),
+        ],
+        compiler_params=pltpu.CompilerParams(vmem_limit_bytes=40 * 2**20),
+        name="panels",
+    )(rows, top, prior[None])
+    return (panel, update[:, :, None, :])
 
 
 def solution(mesh):

time: 232 us -> 111 us (0.48)
  the two profiles are of different devices: /device:TPU:57 before, /device:TPU:1 now
where the time goes in v2:
time: 111 us; the launch traced here: 110 us
  Pallas kernels  105 us (95%)
  local copies, waits for them, and re-layouts  4.5 us (4%)
    pallas_call x1, Pallas kernels, gather_rows(): pl.pallas_call(gather_kernel, out_shape=(jax.ShapeDtypeStruct((2, 16, 4,...  79.2 us
    pallas_call x1, Pallas kernels, on_device(): pl.pallas_call(panel_kernel, out_shape=(jax.ShapeDtypeStruct((1, PANEL, P...  25.8 us
    unnamed x7, local copies, waits for them, and re-layouts  4.5 us

profile of v2, /device:TPU:1, one launch (start us, length us, event | category | flops | bytes accessed | tf_op | source)
XLA Modules:
  0.0 110.1 jit_solution(18170326323361425137)
XLA Ops:
  0.6 0.0 copy-start.2
  0.6 79.2 %reduce_gram.1 = (bf16[2,16,4,32,128]{4,3,2,1,0:T(8,128)(2,1)}, f32[2,16,4,8,256]{4,3,2,1,0:T(8,128)}) custom-call(bf16[512,8192]{1,0:T(8,128)(2,1)} %feat.1), custom_call_target="tpu_custom_call" | custom-call | flops 4294967296 | bytes 10485760 | tf_op jit(solution)/shard_map/reduce_gram/pallas_call | solution.py:313
  79.8 0.0 copy-done.2
  79.8 0.0 copy-start
  79.8 1.2 %copy-done = bf16[2,16,4,32,128]{4,3,2,1,0:T(8,128)(2,1)S(1)} copy-done((bf16[2,16,4,32,128]{4,3,2,1,0:T(8,128)(2,1)S(1)}, bf16[2,16,4,32,128]{4,3,2,1,0:T(8,128)(2,1)}, u32[]{:S(2)}) %copy-start) | copy-done | bytes 1048600
  81.1 0.0 copy-start.1
  81.1 1.2 %copy-done.1 = f32[2,16,4,8,256]{4,3,2,1,0:T(8,128)S(1)} copy-done((f32[2,16,4,8,256]{4,3,2,1,0:T(8,128)S(1)}, f32[2,16,4,8,256]{4,3,2,1,0:T(8,128)}, u32[]{:S(2)}) %copy-start.1) | copy-done | bytes 1048600
  82.3 25.8 %panels.1 = (f32[1,512,512]{2,1,0:T(8,128)}, f32[1,512,512]{2,1,0:T(8,128)S(1)}) custom-call(bf16[2,16,4,32,128]{4,3,2,1,0:T(8,128)(2,1)S(1)} %copy-done, f32[2,16,4,8,256]{4,3,2,1,0:T(8,128)S(1)} %copy-done.1, f32[1,512]{1,0:T(1,128)S(1)} %bitcast.3), custom_call_target="tpu_custom_call" | custom-call | tf_op jit(solution)/shard_map/panels/pallas_call | solution.py:481
  108.1 2.0 %copy.4 = f32[1,512,1,512]{3,2,1,0:T(1,128)} copy(f32[1,512,1,512]{3,1,2,0:T(8,128)S(1)} %bitcast.2) | data formatting | bytes 2097152
Async XLA Ops:
  0.6 79.2 %copy-start.2 = (f32[512]{0:T(512)S(1)}, f32[512]{0:T(512)}, u32[]{:S(2)}) copy-start(f32[512]{0:T(512)} %param.3) | copy-start | bytes 6148
  79.8 1.2 %copy-start = (bf16[2,16,4,32,128]{4,3,2,1,0:T(8,128)(2,1)S(1)}, bf16[2,16,4,32,128]{4,3,2,1,0:T(8,128)(2,1)}, u32[]{:S(2)}) copy-start(bf16[2,16,4,32,128]{4,3,2,1,0:T(8,128)(2,1)} %get-tuple-element.6.rows) | copy-start | bytes 3145732
  81.1 1.2 %copy-start.1 = (f32[2,16,4,8,256]{4,3,2,1,0:T(8,128)S(1)}, f32[2,16,4,8,256]{4,3,2,1,0:T(8,128)}, u32[]{:S(2)}) copy-start(f32[2,16,4,8,256]{4,3,2,1,0:T(8,128)} %get-tuple-element.7.top) | copy-start | bytes 3145732

commit v3 on v2

--- a/solution.py
+++ b/solution.py
@@ -70,7 +70,7 @@
     return (quarter, ya, yb, xb, xa)
 
 
-def gather_kernel(feat, rows_out, top_out, own, theirs, lead_own, lead_their, lead_t, acc, top,
+def panel_kernel(feat, prior, panel_out, other, rows_out, top_out, a, g, work, v, below, inv, lead, rest, own, theirs, lead_own, lead_their, lead_t, acc, top,
                   s0, s1, s2, s3, r0, r1, r2, r3, ts0, ts1, ts2, ts3, tr0, tr1, tr2, tr3,
                   zsend, zrecv, zown, topz,
                   load_sem, feat_send, feat_recv, step_send, step_recv, top_send, top_recv,
@@ -254,13 +254,18 @@
     ]
     for copy in plane:
         copy.start()
-    pltpu.make_async_copy(zrecv.at[pl.ds(0, 7)], zrecv.at[pl.ds(0, 7)], z_recv).wait()
+    top_mate.wait()
+    for h in range(2):
+        for q in range(4):
+            for t in range(16):
+                a[pl.ds(128 * q + 8 * t, 8), pl.ds(BLOCK * h, BLOCK)] = top_out[h, t, q]
+    for b in range(4):
+        at = pl.ds(128 * b, 128)
+        i = lax.broadcasted_iota(jnp.int32, (128, 128), 0)
+        j = lax.broadcasted_iota(jnp.int32, (128, 128), 1)
+        a[at, at] = a[at, at] + jnp.where(i == j, prior[:, at], 0.0)
+
     slot = 8 * me.core + 4 * me.zl + 2 * me.bits["ya"] + me.bits["yb"]
-    for q in range(4):
-        total = zown[me.zl, q]
-        for j in range(1, 8):
-            total = total + zrecv[(me.z + j) % 8, q].astype(F32)
-        rows_out[0, slot, q] = total.astype(rows_out.dtype)
     mine = rows_out.at[0, slot]
     row_copies = [
         exchange(mine, mine, row_send.at[j - 1], row_recv, (me.r, (me.c + j) % 16))
@@ -270,19 +275,63 @@
         exchange(mine, rows_out.at[1, slot], col_send.at[j], col_recv, ((me.r + j) % 16, me.r))
         for j in range(16)
     ]
-    for j in range(1, 16):
-        col_copies[j].start()
-        row_copies[j - 1].start()
-
-    @pl.when(me.r != me.c)
-    def _():
-        col_copies[0].start()
-
-    @pl.when(me.r == me.c)
-    def _():
-        rows_out[1, slot] = rows_out[0, slot]
-
-    top_mate.wait()
+
+    def finish_z():
+        pltpu.make_async_copy(zrecv.at[pl.ds(0, 7)], zrecv.at[pl.ds(0, 7)], z_recv).wait()
+        for q in range(4):
+            total = zown[me.zl, q]
+            for j in range(1, 8):
+                total = total + zrecv[(me.z + j) % 8, q].astype(F32)
+            rows_out[0, slot, q] = total.astype(rows_out.dtype)
+        for j in range(1, 16):
+            col_copies[j].start()
+            row_copies[j - 1].start()
+
+        @pl.when(me.r != me.c)
+        def _():
+            col_copies[0].start()
+
+        @pl.when(me.r == me.c)
+        def _():
+            rows_out[1, slot] = rows_out[0, slot]
+
+    def second_tile(tile):
+        below[...] = dot_t(tile[128:BLOCK, :128], v[0])
+        work[...] = tile[128:BLOCK, 128:BLOCK] - dot_t(below[...], below[...])
+
+    def finish_inverse(half):
+        inv[half, :128, :128] = v[0]
+        inv[half, :128, 128:] = jnp.zeros((128, 128), F32)
+        inv[half, 128:, :128] = -dot(v[1], dot(below[...], v[0]))
+        inv[half, 128:, 128:] = v[1]
+
+    def factorise(b, carry):
+        @pl.when(b == 0)
+        def _():
+            work[...] = a[:128, :128]
+
+        @pl.when(b == 1)
+        def _():
+            finish_z()
+            second_tile(a)
+
+        @pl.when(b == 2)
+        def _():
+            finish_inverse(0)
+            lead[...] = dot_t(a[BLOCK:, :BLOCK], inv[0])
+            rest[...] = a[BLOCK:, BLOCK:] - dot_t(lead[...], lead[...])
+            work[...] = rest[:128, :128]
+
+        @pl.when(b == 3)
+        def _():
+            second_tile(rest)
+
+        v[b % 2] = inverse_128(work[...])
+        return carry
+
+    lax.fori_loop(0, 4, factorise, 0)
+    finish_inverse(1)
+
     fifteen = rows_out.at[0, pl.ds(0, 15)]
     pltpu.make_async_copy(fifteen, fifteen, row_recv).wait()
 
@@ -295,6 +344,34 @@
     def _():
         pltpu.make_async_copy(fifteen, fifteen, col_recv).wait()
 
+    for side in range(2):
+        for h in range(2):
+            for zl in range(2):
+                for t in range(4):
+                    for q in range(4):
+                        g[side, pl.ds(128 * q + 32 * t, 32), pl.ds(BLOCK * h + 128 * zl, 128)] = (
+                            rows_out[side, 8 * h + 4 * zl + t, q].astype(F32)
+                        )
+        for b in range(2):
+
+            @pl.when((me.r, me.c)[side] == b)
+            def _():
+                g[side, :, :BLOCK] = a[:, pl.ds(BLOCK * b, BLOCK)]
+
+    for b in range(2):
+        at = pl.ds(BLOCK * b, BLOCK)
+        first = dot_t(g[0, :BLOCK, at].T, inv[0])
+        second = dot_t(g[0, BLOCK:, at].T - dot_t(first, lead[...]), inv[1])
+        if b == 0:
+            second = jnp.where(me.r == 0, 0.0, second)
+        panel_out[at, :BLOCK] = first
+        panel_out[at, BLOCK:] = second
+    first = dot(inv[0], g[1, :BLOCK])
+    second = dot(inv[1], g[1, BLOCK:] - dot(lead[...], first))
+    other[:BLOCK] = first.astype(jnp.bfloat16)
+    other[BLOCK:, :BLOCK] = jnp.where(me.c == 0, 0.0, second[:, :BLOCK]).astype(jnp.bfloat16)
+    other[BLOCK:, BLOCK:] = second[:, BLOCK:].astype(jnp.bfloat16)
+
     for copies in (row_copies, col_copies[1:], plane, top_plane, top_gather, shares):
         for copy in copies:
             copy.wait_send()
@@ -305,20 +382,30 @@
                 main_copy(step, zh, q).wait_send()
 
 
-def gather_rows(features):
+def panels(features, prior):
     twos = lambda n: (2,) * n
     wire = lambda n: pltpu.VMEM((4, 4) + twos(n) + (32, BLOCK), WIRE)
     exact = lambda n: pltpu.VMEM((4,) + twos(n) + (8, BLOCK), F32)
     dma = pltpu.SemaphoreType.DMA
     return pl.pallas_call(
-        gather_kernel,
+        panel_kernel,
         out_shape=(
-            jax.ShapeDtypeStruct((2, 16, 4, 32, 128), WIRE),
-            jax.ShapeDtypeStruct((2, 16, 4, 8, BLOCK), F32),
+            jax.ShapeDtypeStruct((PANEL, PANEL), F32),
+            jax.ShapeDtypeStruct((PANEL, PANEL), jnp.bfloat16),
         ),
-        in_specs=[pl.BlockSpec(memory_space=pl.ANY)],
+        in_specs=[pl.BlockSpec(memory_space=pl.ANY), pl.BlockSpec(memory_space=pltpu.VMEM)],
         out_specs=(pl.BlockSpec(memory_space=pltpu.VMEM),) * 2,
         scratch_shapes=[
+            pltpu.VMEM((2, 16, 4, 32, 128), WIRE),
+            pltpu.VMEM((2, 16, 4, 8, BLOCK), F32),
+            pltpu.VMEM((PANEL, PANEL), F32),
+            pltpu.VMEM((2, PANEL, PANEL), F32),
+            pltpu.VMEM((128, 128), F32),
+            pltpu.VMEM((2, 128, 128), F32),
+            pltpu.VMEM((128, 128), F32),
+            pltpu.VMEM((2, BLOCK, BLOCK), F32),
+            pltpu.VMEM((BLOCK, BLOCK), F32),
+            pltpu.VMEM((BLOCK, BLOCK), F32),
             pltpu.VMEM((TOKENS, HALF), jnp.bfloat16),
             pltpu.VMEM((TOKENS, HALF), jnp.bfloat16),
             pltpu.VMEM((TOKENS, PANEL), jnp.bfloat16),
@@ -345,8 +432,8 @@
         cost_estimate=pl.CostEstimate(
             flops=2 * PANEL * 1024 * HALF, bytes_accessed=10 * 2**20, transcendentals=0
         ),
-        name="reduce_gram",
-    )(features)
+        name="panels",
+    )(features, prior)
 
 
 def lane(tile, k):
@@ -416,87 +503,31 @@
     )
 
 
-def inverse_256(ref, start, out):
-    lo, hi = pl.ds(start, 128), pl.ds(start + 128, 128)
-    v1 = inverse_128(ref[lo, lo])
-    below = dot_t(ref[hi, lo], v1)
-    v2 = inverse_128(ref[hi, hi] - dot_t(below, below))
-    out[:128, :128] = v1
-    out[:128, 128:] = jnp.zeros((128, 128), F32)
-    out[128:, :128] = -dot(v2, dot(below, v1))
-    out[128:, 128:] = v2
-
-
-def panel_kernel(rows, top, prior, panel_out, update_out, a, g, inv1, inv2, other):
-    r, c = lax.axis_index("row"), lax.axis_index("col")
-    for h in range(2):
-        for q in range(4):
-            for s in range(16):
-                a[pl.ds(128 * q + 8 * s, 8), pl.ds(BLOCK * h, BLOCK)] = top[h, s, q]
-    for b in range(4):
-        at = pl.ds(128 * b, 128)
-        i = lax.broadcasted_iota(jnp.int32, (128, 128), 0)
-        j = lax.broadcasted_iota(jnp.int32, (128, 128), 1)
-        a[at, at] = a[at, at] + jnp.where(i == j, prior[:, at], 0.0)
-    for side in range(2):
-        for h in range(2):
-            for zl in range(2):
-                for s in range(4):
-                    for q in range(4):
-                        g[side, pl.ds(128 * q + 32 * s, 32), pl.ds(BLOCK * h + 128 * zl, 128)] = rows[
-                            side, 8 * h + 4 * zl + s, q
-                        ].astype(F32)
-        own = (r, c)[side]
-        for b in range(2):
-
-            @pl.when(own == b)
-            def _():
-                g[side, :, :BLOCK] = a[:, pl.ds(BLOCK * b, BLOCK)]
-
-    inverse_256(a, 0, inv1)
-    lead = dot_t(a[BLOCK:, :BLOCK], inv1[...])
-    a[BLOCK:, BLOCK:] = a[BLOCK:, BLOCK:] - dot_t(lead, lead)
-    inverse_256(a, BLOCK, inv2)
-
-    for b in range(2):
-        at = pl.ds(BLOCK * b, BLOCK)
-        first = dot_t(g[0, :BLOCK, at].T, inv1[...])
-        second = dot_t(g[0, BLOCK:, at].T - dot_t(first, lead), inv2[...])
-        if b == 0:
-            second = jnp.where(r == 0, 0.0, second)
-        panel_out[0, at, :BLOCK] = first
-        panel_out[0, at, BLOCK:] = second
-    first = dot(inv1[...], g[1, :BLOCK])
-    second = dot(inv2[...], g[1, BLOCK:] - dot(lead, first))
-    other[:BLOCK] = first.astype(jnp.bfloat16)
-    other[BLOCK:, :BLOCK] = jnp.where(c == 0, 0.0, second[:, :BLOCK]).astype(jnp.bfloat16)
-    other[BLOCK:, BLOCK:] = second[:, BLOCK:].astype(jnp.bfloat16)
-    update_out[0] = jnp.dot(
-        panel_out[0].astype(jnp.bfloat16), other[...], preferred_element_type=F32
+def finish_kernel(panel, other, panel_out, update_out, product, sem):
+    panel_copy = pltpu.make_async_copy(panel, panel_out.at[0], sem.at[0])
+    panel_copy.start()
+    product[...] = jnp.dot(
+        panel[...].astype(jnp.bfloat16), other[...], preferred_element_type=F32
     ) * (1.0 / PANEL)
+    product_copy = pltpu.make_async_copy(product, update_out.at[0, :, 0, :], sem.at[1])
+    product_copy.start()
+    panel_copy.wait()
+    product_copy.wait()
 
 
 def on_device(features, prior):
-    rows, top = gather_rows(features)
-    panel, update = pl.pallas_call(
-        panel_kernel,
+    panel, other = panels(features, prior[None])
+    return pl.pallas_call(
+        finish_kernel,
         out_shape=(
             jax.ShapeDtypeStruct((1, PANEL, PANEL), F32),
-            jax.ShapeDtypeStruct((1, PANEL, PANEL), F32),
+            jax.ShapeDtypeStruct((1, PANEL, 1, PANEL), F32),
         ),
-        in_specs=[pl.BlockSpec(memory_space=pltpu.VMEM)] * 3,
-        out_specs=(pl.BlockSpec(memory_space=pltpu.VMEM),) * 2,
-        scratch_shapes=[
-            pltpu.VMEM((PANEL, PANEL), F32),
-            pltpu.VMEM((2, PANEL, PANEL), F32),
-            pltpu.VMEM((BLOCK, BLOCK), F32),
-            pltpu.VMEM((BLOCK, BLOCK), F32),
-            pltpu.VMEM((PANEL, PANEL), jnp.bfloat16),
-        ],
-        compiler_params=pltpu.CompilerParams(vmem_limit_bytes=40 * 2**20),
-        name="panels",
-    )(rows, top, prior[None])
-    return (panel, update[:, :, None, :])
+        in_specs=[pl.BlockSpec(memory_space=pltpu.VMEM)] * 2,
+        out_specs=(pl.BlockSpec(memory_space=pl.ANY),) * 2,
+        scratch_shapes=[pltpu.VMEM((PANEL, PANEL), F32), pltpu.SemaphoreType.DMA((2,))],
+        name="product",
+    )(panel, other)
 
 
 def solution(mesh):

time: 111 us -> 90.1 us (0.81)
  the two profiles are of different devices: /device:TPU:1 before, /device:TPU:2 now
where the time goes in v3:
time: 90.1 us; the launch traced here: 90 us
  Pallas kernels  89.2 us (99%)
    pallas_call x1, Pallas kernels, panels(): pl.pallas_call(panel_kernel, out_shape=(jax.ShapeDtypeStruct((PANEL, PANE...  86.4 us
    pallas_call x1, Pallas kernels, on_device(): pl.pallas_call(finish_kernel, out_shape=(jax.ShapeDtypeStruct((1, PANEL,...  2.79 us

profile of v3, /device:TPU:2, one launch (start us, length us, event | category | flops | bytes accessed | tf_op | source)
XLA Modules:
  0.0 90.0 jit_solution(9810614682254920097)
XLA Ops:
  0.6 86.4 %panels.1 = (f32[512,512]{1,0:T(8,128)}, bf16[512,512]{1,0:T(8,128)(2,1)}) custom-call(bf16[512,8192]{1,0:T(8,128)(2,1)} %feat.1, f32[1,512]{1,0:T(1,128)} %bitcast.1), custom_call_target="tpu_custom_call" | custom-call | flops 4294967296 | bytes 10485760 | tf_op jit(solution)/shard_map/panels/pallas_call | solution.py:390
  87.1 2.8 %product.1 = (f32[1,512,512]{2,1,0:T(8,128)}, f32[1,512,1,512]{3,2,1,0:T(1,128)}) custom-call(f32[512,512]{1,0:T(8,128)} %get-tuple-element.4.panel, bf16[512,512]{1,0:T(8,128)(2,1)} %get-tuple-element.5.other), custom_call_target="tpu_custom_call" | custom-call | tf_op jit(solution)/shard_map/product/pallas_call | solution.py:520

commit v4 on v3

--- a/solution.py
+++ b/solution.py
@@ -20,6 +20,8 @@
     ("yb", "xa", "xb", "ya"),
 )
 FULL = slice(None)
+TOP_WAVES = {3: 1, 5: 2}
+LAST_WAVE, END_Z, PASS = (0, 4), (1, 0), (3, 12)
 
 
 class Place:
@@ -65,20 +67,22 @@
     return (zh, pick("xb"), pick("xa"), quarter, pick("ya"), pick("yb"))
 
 
-def top_index(place, quarter, step, last):
-    _, xb, xa, _, ya, yb = tile_index(place, quarter, 0, step, last)
-    return (quarter, ya, yb, xb, xa)
-
-
-def panel_kernel(feat, prior, panel_out, other, rows_out, top_out, a, g, work, v, below, inv, lead, rest, own, theirs, lead_own, lead_their, lead_t, acc, top,
-                  s0, s1, s2, s3, r0, r1, r2, r3, ts0, ts1, ts2, ts3, tr0, tr1, tr2, tr3,
+def strip(y):
+    return 2 * (((y + 1) // 2) % 2) + y // 2
+
+
+def top_slot(x, y):
+    return 4 * strip(y) + 2 * (x // 2) + ((x + 1) // 2) % 2
+
+
+def panel_kernel(feat, prior, panel_out, other, rows_out, top_out, a, g, work, v, below, inv, lead, rest, own, theirs, lead_own, lead_their, lead_t, acc, top, top_parts,
+                  s0, s1, s2, s3, r0, r1, r2, r3,
                   zsend, zrecv, zown, topz,
-                  load_sem, feat_send, feat_recv, step_send, step_recv, top_send, top_recv,
+                  load_sem, feat_send, feat_recv, step_send, step_recv, ts_send, ts_recv,
                   z_send, z_recv, tz_send, tz_recv, tg_send, tg_recv, core_send, core_recv,
-                  row_send, row_recv, col_send, col_recv):
+                  row_send, row_recv, col_send, col_recv, pass_send, pass_recv):
     me = Place()
     sends, recvs = (s0, s1, s2, s3), (r0, r1, r2, r3)
-    tsends, trecvs = (ts0, ts1, ts2, ts3), (tr0, tr1, tr2, tr3)
     mate = me.at(core=1 - me.core)
     loads = [pltpu.make_async_copy(feat.at[:, pl.ds(0, PANEL)], lead_own, load_sem.at[0])]
     for i in range(4):
@@ -98,11 +102,11 @@
         pl.semaphore_signal(barrier, inc=1, device_id=device, device_id_type=MESH)
 
     greet(mate)
-    for dim in ORDERS[0]:
-        greet(me.partner(dim))
+    for j in range(1, 16):
+        greet(me.at(x=(me.x + j) % 4, y=(me.y + j // 4) % 4))
     for j in range(1, 8):
         greet(me.at(z=(me.z + j) % 8))
-    pl.semaphore_wait(barrier, 12)
+    pl.semaphore_wait(barrier, 23)
 
     shares = [
         pltpu.make_async_remote_copy(
@@ -134,30 +138,15 @@
         )
 
     lanes = pl.ds(pl.multiple_of(me.core * BLOCK, BLOCK), BLOCK)
-    top[...] = products(lead_own[:, lanes], lead_their[:, lanes]).reshape(4, 2, 2, 2, 2, 8, BLOCK)
+    square = products(lead_own[:, lanes], lead_their[:, lanes]).reshape(4, 16, 8, BLOCK)
+    for t in range(16):
+        top[t] = square[:, t]
 
     def exchange(src, dst, send, recv, device):
         return pltpu.make_async_remote_copy(
             src_ref=src, dst_ref=dst, send_sem=send, recv_sem=recv,
             device_id=device, device_id_type=MESH,
         )
-
-    def top_copy(step, q):
-        return exchange(
-            tsends[step].at[q], trecvs[step].at[q], top_send.at[step, q], top_recv.at[step, q],
-            me.partner(ORDERS[q][step]),
-        )
-
-    def top_start(step):
-        for q in range(4):
-            tsends[step][q] = top[top_index(me, q, step, False)]
-            top_copy(step, q).start()
-
-    def top_finish(step):
-        for q in range(4):
-            top_copy(step, q).wait_recv()
-            at = top_index(me, q, step, True)
-            top[at] = top[at] + trecvs[step][q]
 
     def main_copy(step, zh, q):
         return exchange(
@@ -190,71 +179,82 @@
 
         lax.fori_loop(0, 4, body, 0)
 
-    my_top = (me.bits["ya"], me.bits["yb"], me.bits["xb"], me.bits["xa"])
-    my_slot = 8 * my_top[0] + 4 * my_top[1] + 2 * my_top[2] + my_top[3]
-    top_start(0)
-    for wave in range(8):
-        if wave >= 1 and wave <= 4:
-            top_finish(wave - 1)
-            if wave < 4:
-                top_start(wave)
-            else:
-                for q in range(4):
-                    topz[me.z, q] = top[(q,) + my_top]
-                top_plane = [
-                    exchange(topz.at[me.z], topz.at[me.z], tz_send.at[j - 1], tz_recv,
-                             me.at(z=(me.z + j) % 8))
-                    for j in range(1, 8)
-                ]
-                for copy in top_plane:
-                    copy.start()
-        if wave < 4:
-            multiply(wave)
-            main_start(0, wave)
-        if wave == 5:
-            pltpu.make_async_copy(topz.at[pl.ds(0, 7)], topz.at[pl.ds(0, 7)], tz_recv).wait()
-            for q in range(4):
-                total = topz[0, q]
-                for z in range(1, 8):
-                    total = total + topz[z, q]
-                top_out[me.core, my_slot, q] = total
-            top_gather = [
-                exchange(top_out.at[me.core, my_slot], top_out.at[me.core, my_slot],
-                         tg_send.at[j - 1], tg_recv,
-                         me.at(x=(me.x + j) % 4, y=(me.y + j // 4) % 4))
-                for j in range(1, 16)
-            ]
+    my_slot = top_slot(me.x, me.y)
+    plane_at = [((me.x + j) % 4, (me.y + j // 4) % 4) for j in range(1, 16)]
+    top_sums = [
+        exchange(top.at[top_slot(x, y)], top_parts.at[my_slot], ts_send.at[j], ts_recv, me.at(x=x, y=y))
+        for j, (x, y) in enumerate(plane_at)
+    ]
+    top_column = [
+        exchange(topz.at[me.z], topz.at[me.z], tz_send.at[j - 1], tz_recv, me.at(z=(me.z + j) % 8))
+        for j in range(1, 8)
+    ]
+    top_gather = [
+        exchange(top_out.at[me.core, my_slot], top_out.at[me.core, my_slot],
+                 tg_send.at[j], tg_recv.at[(j + 1) // 4], me.at(x=x, y=y))
+        for j, (x, y) in enumerate(plane_at)
+    ]
+    top_pass = []
+    for k in range(4):
+        four = top_out.at[me.core, pl.ds(4 * strip((me.y + 4 - k) % 4), 4)]
+        top_pass.append(exchange(four, four, core_send.at[k], core_recv.at[k], mate))
+
+    def top_stage(stage):
+        if stage == 0:
+            for copy in top_sums:
+                copy.start()
+        if stage == 1:
+            fifteen = top_parts.at[pl.ds(0, 15)]
+            pltpu.make_async_copy(fifteen, fifteen, ts_recv).wait()
+            top_parts[my_slot] = top[my_slot]
+            topz[me.z] = pair_sum([top_parts[t] for t in range(16)])
+            for copy in top_column:
+                copy.start()
+        if stage == 2:
+            seven = topz.at[pl.ds(0, 7)]
+            pltpu.make_async_copy(seven, seven, tz_recv).wait()
+            top_out[me.core, my_slot] = pair_sum([topz[z] for z in range(8)])
             for copy in top_gather:
                 copy.start()
+        if stage == 3:
+            for k in range(4):
+                some = top_out.at[me.core, pl.ds(0, 4 if k else 3)]
+                pltpu.make_async_copy(some, some, tg_recv.at[k]).wait()
+                top_pass[k].start()
+
+    home = lambda q, zh: (zh, me.bits["xb"], me.bits["xa"], q, me.bits["ya"], me.bits["yb"])
+    column = [exchange(zsend.at[z], zrecv.at[me.z], z_send.at[z], z_recv, me.at(z=z)) for z in range(8)]
+
+    def send_strips(zh):
+        for q in range(4):
+            tile = acc[home(q, zh)]
+            for zl in range(2):
+                zsend[zh * 2 + zl, q] = tile[:, zl * 128 : zl * 128 + 128].astype(WIRE)
+        for z in (2 * zh, 2 * zh + 1):
+            pl.when(me.z != z)(column[z].start)
+
+    def wave(number):
+        if number < 4:
+            multiply(number)
+            main_start(0, number)
         for step in range(4):
-            zh = wave - step - 1
+            zh = number - step - 1
             if 0 <= zh < 4:
                 main_finish(step, zh)
                 if step < 3:
                     main_start(step + 1, zh)
-        if wave == 6:
-            fifteen = top_out.at[me.core, pl.ds(0, 15)]
-            pltpu.make_async_copy(fifteen, fifteen, tg_recv).wait()
-            top_mate = exchange(top_out.at[me.core], top_out.at[me.core], core_send, core_recv, mate)
-            top_mate.start()
-
-    home = lambda q, zh: (zh, me.bits["xb"], me.bits["xa"], q, me.bits["ya"], me.bits["yb"])
-    for q in range(4):
-        for zh in range(4):
-            tile = acc[home(q, zh)]
-            for zl in range(2):
-                zsend[zh * 2 + zl, q] = tile[:, zl * 128 : zl * 128 + 128].astype(WIRE)
-        tile = acc[home(q, me.zh)]
-        for zl in range(2):
-            zown[zl, q] = tile[:, zl * 128 : zl * 128 + 128]
-    plane = [
-        exchange(zsend.at[(me.z + j) % 8], zrecv.at[me.z], z_send.at[j - 1], z_recv,
-                 me.at(z=(me.z + j) % 8))
-        for j in range(1, 8)
-    ]
-    for copy in plane:
-        copy.start()
-    top_mate.wait()
+                else:
+                    send_strips(zh)
+
+    top_stage(0)
+    for number in range(7):
+        if number in TOP_WAVES:
+            top_stage(TOP_WAVES[number])
+        wave(number)
+    top_stage(3)
+
+    for copy in top_pass:
+        copy.wait_recv()
     for h in range(2):
         for q in range(4):
             for t in range(16):
@@ -263,29 +263,38 @@
         at = pl.ds(128 * b, 128)
         i = lax.broadcasted_iota(jnp.int32, (128, 128), 0)
         j = lax.broadcasted_iota(jnp.int32, (128, 128), 1)
-        a[at, at] = a[at, at] + jnp.where(i == j, prior[:, at], 0.0)
+        a[at, at] = a[at, at] + jnp.where(i == j, prior[at].reshape(1, 128), 0.0)
 
     slot = 8 * me.core + 4 * me.zl + 2 * me.bits["ya"] + me.bits["yb"]
     mine = rows_out.at[0, slot]
     row_copies = [
-        exchange(mine, mine, row_send.at[j - 1], row_recv, (me.r, (me.c + j) % 16))
-        for j in range(1, 16)
+        exchange(mine, mine, row_send.at[j - 1], row_recv,
+                 me.at(y=(me.y + j) % 4, z=2 * me.zh + (me.zl + j // 4) % 2))
+        for j in range(1, 8)
     ]
+    eight = rows_out.at[0, pl.ds(8 * me.core, 8)]
+    row_pass = exchange(eight, eight, pass_send, pass_recv, mate)
     col_copies = [
         exchange(mine, rows_out.at[1, slot], col_send.at[j], col_recv, ((me.r + j) % 16, me.r))
         for j in range(16)
     ]
 
+    def last_wave():
+        wave(7)
+
     def finish_z():
+        for q in range(4):
+            tile = acc[home(q, me.zh)]
+            for zl in range(2):
+                zown[zl, q] = tile[:, zl * 128 : zl * 128 + 128]
         pltpu.make_async_copy(zrecv.at[pl.ds(0, 7)], zrecv.at[pl.ds(0, 7)], z_recv).wait()
         for q in range(4):
             total = zown[me.zl, q]
             for j in range(1, 8):
                 total = total + zrecv[(me.z + j) % 8, q].astype(F32)
             rows_out[0, slot, q] = total.astype(rows_out.dtype)
-        for j in range(1, 16):
-            col_copies[j].start()
-            row_copies[j - 1].start()
+        for copy in row_copies + col_copies[1:]:
+            copy.start()
 
         @pl.when(me.r != me.c)
         def _():
@@ -305,6 +314,11 @@
         inv[half, 128:, :128] = -dot(v[1], dot(below[...], v[0]))
         inv[half, 128:, 128:] = v[1]
 
+    def pass_rows():
+        seven = rows_out.at[0, pl.ds(0, 7)]
+        pltpu.make_async_copy(seven, seven, row_recv).wait()
+        row_pass.start()
+
     def factorise(b, carry):
         @pl.when(b == 0)
         def _():
@@ -312,7 +326,6 @@
 
         @pl.when(b == 1)
         def _():
-            finish_z()
             second_tile(a)
 
         @pl.when(b == 2)
@@ -326,25 +339,18 @@
         def _():
             second_tile(rest)
 
-        v[b % 2] = inverse_128(work[...])
+        def between(panel):
+            for when, act in ((LAST_WAVE, last_wave), (END_Z, finish_z), (PASS, pass_rows)):
+                if panel == when[1]:
+                    pl.when(b == when[0])(act)
+
+        v[b % 2] = inverse_128(work[...], between)
         return carry
 
     lax.fori_loop(0, 4, factorise, 0)
     finish_inverse(1)
 
-    fifteen = rows_out.at[0, pl.ds(0, 15)]
-    pltpu.make_async_copy(fifteen, fifteen, row_recv).wait()
-
-    @pl.when(me.r != me.c)
-    def _():
-        pltpu.make_async_copy(rows_out.at[1], rows_out.at[1], col_recv).wait()
-        col_copies[0].wait_send()
-
-    @pl.when(me.r == me.c)
-    def _():
-        pltpu.make_async_copy(fifteen, fifteen, col_recv).wait()
-
-    for side in range(2):
+    def assemble(side):
         for h in range(2):
             for zl in range(2):
                 for t in range(4):
@@ -358,6 +364,8 @@
             def _():
                 g[side, :, :BLOCK] = a[:, pl.ds(BLOCK * b, BLOCK)]
 
+    row_pass.wait_recv()
+    assemble(0)
     for b in range(2):
         at = pl.ds(BLOCK * b, BLOCK)
         first = dot_t(g[0, :BLOCK, at].T, inv[0])
@@ -366,18 +374,34 @@
             second = jnp.where(me.r == 0, 0.0, second)
         panel_out[at, :BLOCK] = first
         panel_out[at, BLOCK:] = second
+
+    @pl.when(me.r != me.c)
+    def _():
+        pltpu.make_async_copy(rows_out.at[1], rows_out.at[1], col_recv).wait()
+        col_copies[0].wait_send()
+
+    @pl.when(me.r == me.c)
+    def _():
+        fifteen = rows_out.at[1, pl.ds(0, 15)]
+        pltpu.make_async_copy(fifteen, fifteen, col_recv).wait()
+
+    assemble(1)
     first = dot(inv[0], g[1, :BLOCK])
     second = dot(inv[1], g[1, BLOCK:] - dot(lead[...], first))
     other[:BLOCK] = first.astype(jnp.bfloat16)
     other[BLOCK:, :BLOCK] = jnp.where(me.c == 0, 0.0, second[:, :BLOCK]).astype(jnp.bfloat16)
     other[BLOCK:, BLOCK:] = second[:, BLOCK:].astype(jnp.bfloat16)
 
-    for copies in (row_copies, col_copies[1:], plane, top_plane, top_gather, shares):
+    for copies in (row_copies, col_copies[1:], shares, [row_pass]):
+        for copy in copies:
+            copy.wait_send()
+    for z in range(8):
+        pl.when(me.z != z)(column[z].wait_send)
+    for copies in (top_sums, top_column, top_gather, top_pass):
         for copy in copies:
             copy.wait_send()
     for step in range(4):
         for q in range(4):
-            top_copy(step, q).wait_send()
             for zh in range(4):
                 main_copy(step, zh, q).wait_send()
 
@@ -385,7 +409,6 @@
 def panels(features, prior):
     twos = lambda n: (2,) * n
     wire = lambda n: pltpu.VMEM((4, 4) + twos(n) + (32, BLOCK), WIRE)
-    exact = lambda n: pltpu.VMEM((4,) + twos(n) + (8, BLOCK), F32)
     dma = pltpu.SemaphoreType.DMA
     return pl.pallas_call(
         panel_kernel,
@@ -412,19 +435,18 @@
             pltpu.VMEM((TOKENS, PANEL), jnp.bfloat16),
             pltpu.VMEM((PANEL, 2 * TOKENS), jnp.bfloat16),
             pltpu.VMEM((4, 2, 2, 4, 2, 2, 32, BLOCK), F32),
-            pltpu.VMEM((4, 2, 2, 2, 2, 8, BLOCK), F32),
+            pltpu.VMEM((16, 4, 8, BLOCK), F32),
+            pltpu.VMEM((16, 4, 8, BLOCK), F32),
             *[wire(n) for n in (3, 2, 1, 0)],
             *[wire(n) for n in (3, 2, 1, 0)],
-            *[exact(n) for n in (3, 2, 1, 0)],
-            *[exact(n) for n in (3, 2, 1, 0)],
             pltpu.VMEM((8, 4, 32, 128), WIRE),
             pltpu.VMEM((8, 4, 32, 128), WIRE),
             pltpu.VMEM((2, 4, 32, 128), F32),
             pltpu.VMEM((8, 4, 8, BLOCK), F32),
             dma((5,)), dma((5,)), dma((5,)),
-            dma((4, 4, 4)), dma((4, 4, 4)), dma((4, 4)), dma((4, 4)),
-            dma((7,)), dma, dma((7,)), dma, dma((15,)), dma, dma, dma,
-            dma((15,)), dma, dma((16,)), dma,
+            dma((4, 4, 4)), dma((4, 4, 4)), dma((15,)), dma,
+            dma((8,)), dma, dma((7,)), dma, dma((15,)), dma((4,)), dma((4,)), dma((4,)),
+            dma((7,)), dma, dma((16,)), dma, dma, dma,
         ],
         compiler_params=pltpu.CompilerParams(
             collective_id=1, has_side_effects=True, vmem_limit_bytes=56 * 2**20
@@ -450,7 +472,7 @@
     return terms[0]
 
 
-def inverse_128(tile):
+def inverse_128(tile, between):
     s = [tile[8 * i : 8 * i + 8] for i in range(16)]
     rows = lax.broadcasted_iota(jnp.int32, (8, 128), 0)
     cols = lax.broadcasted_iota(jnp.int32, (8, 128), 1)
@@ -464,6 +486,7 @@
         return whole
 
     for p in range(16):
+        between(p)
         near = list(range(p, min(16, p + 2)))
         m = [[lane(s[g], 8 * p + k) for k in range(8)] for g in near]
         us, vs = [], []
@@ -516,7 +539,7 @@
 
 
 def on_device(features, prior):
-    panel, other = panels(features, prior[None])
+    panel, other = panels(features, prior)
     return pl.pallas_call(
         finish_kernel,
         out_shape=(

time: 90.1 us -> 88 us (0.977)
  the two profiles are of different devices: /device:TPU:2 before, /device:TPU:1 now
where the time goes in v4:
time: 88 us; the launch traced here: 87.8 us
  Pallas kernels  87 us (99%)
    pallas_call x1, Pallas kernels, panels(): pl.pallas_call(panel_kernel, out_shape=(jax.ShapeDtypeStruct((PANEL, PANE...  84.2 us
    pallas_call x1, Pallas kernels, on_device(): pl.pallas_call(finish_kernel, out_shape=(jax.ShapeDtypeStruct((1, PANEL,...  2.79 us

profile of v4, /device:TPU:1, one launch (start us, length us, event | category | flops | bytes accessed | tf_op | source)
XLA Modules:
  0.0 87.8 jit_solution(16925311921744696727)
XLA Ops:
  0.6 84.2 %panels.1 = (f32[512,512]{1,0:T(8,128)}, bf16[512,512]{1,0:T(8,128)(2,1)}) custom-call(bf16[512,8192]{1,0:T(8,128)(2,1)} %feat.1, f32[512]{0:T(512)} %prior.1), custom_call_target="tpu_custom_call" | custom-call | flops 4294967296 | bytes 10485760 | tf_op jit(solution)/shard_map/panels/pallas_call | solution.py:413
  84.9 2.8 %product.1 = (f32[1,512,512]{2,1,0:T(8,128)}, f32[1,512,1,512]{3,2,1,0:T(1,128)}) custom-call(f32[512,512]{1,0:T(8,128)} %get-tuple-element.4.panel, bf16[512,512]{1,0:T(8,128)(2,1)} %get-tuple-element.5.other), custom_call_target="tpu_custom_call" | custom-call | tf_op jit(solution)/shard_map/product/pallas_call | solution.py:543

commit v5 on v4

--- a/solution.py
+++ b/solution.py
@@ -132,13 +132,20 @@
     shares[0].wait_recv()
     lead_t[:, TOKENS:] = lead_their[...].T
 
-    def products(left, right):
-        return jnp.dot(lead_t[:, :TOKENS], left, preferred_element_type=F32) + jnp.dot(
-            lead_t[:, TOKENS:], right, preferred_element_type=F32
+    def products(left, right, rows=FULL):
+        return jnp.dot(lead_t[rows, :TOKENS], left, preferred_element_type=F32) + jnp.dot(
+            lead_t[rows, TOKENS:], right, preferred_element_type=F32
         )
 
     lanes = pl.ds(pl.multiple_of(me.core * BLOCK, BLOCK), BLOCK)
-    square = products(lead_own[:, lanes], lead_their[:, lanes]).reshape(4, 16, 8, BLOCK)
+    rows = pl.ds(pl.multiple_of(BLOCK + 128 * me.core, 128), 128)
+    square = jnp.concatenate(
+        [
+            products(lead_own[:, lanes], lead_their[:, lanes], lanes),
+            products(lead_own[:, :BLOCK], lead_their[:, :BLOCK], rows),
+        ],
+        0,
+    ).reshape(3, 16, 8, BLOCK)
     for t in range(16):
         top[t] = square[:, t]
 
@@ -256,9 +263,10 @@
     for copy in top_pass:
         copy.wait_recv()
     for h in range(2):
-        for q in range(4):
+        for q in range(3):
+            start, side = ((128 * q, 0), ((384, 0) if q == 2 else (BLOCK + 128 * q, BLOCK)))[h]
             for t in range(16):
-                a[pl.ds(128 * q + 8 * t, 8), pl.ds(BLOCK * h, BLOCK)] = top_out[h, t, q]
+                a[pl.ds(start + 8 * t, 8), pl.ds(side, BLOCK)] = top_out[h, t, q]
     for b in range(4):
         at = pl.ds(128 * b, 128)
         i = lax.broadcasted_iota(jnp.int32, (128, 128), 0)
@@ -362,7 +370,8 @@
 
             @pl.when((me.r, me.c)[side] == b)
             def _():
-                g[side, :, :BLOCK] = a[:, pl.ds(BLOCK * b, BLOCK)]
+                g[side, :BLOCK, :BLOCK] = a[BLOCK:, :BLOCK].T if b else a[:BLOCK, :BLOCK]
+                g[side, BLOCK:, :BLOCK] = a[BLOCK:, pl.ds(BLOCK * b, BLOCK)]
 
     row_pass.wait_recv()
     assemble(0)
@@ -420,7 +429,7 @@
         out_specs=(pl.BlockSpec(memory_space=pltpu.VMEM),) * 2,
         scratch_shapes=[
             pltpu.VMEM((2, 16, 4, 32, 128), WIRE),
-            pltpu.VMEM((2, 16, 4, 8, BLOCK), F32),
+            pltpu.VMEM((2, 16, 3, 8, BLOCK), F32),
             pltpu.VMEM((PANEL, PANEL), F32),
             pltpu.VMEM((2, PANEL, PANEL), F32),
             pltpu.VMEM((128, 128), F32),
@@ -435,14 +444,14 @@
             pltpu.VMEM((TOKENS, PANEL), jnp.bfloat16),
             pltpu.VMEM((PANEL, 2 * TOKENS), jnp.bfloat16),
             pltpu.VMEM((4, 2, 2, 4, 2, 2, 32, BLOCK), F32),
-            pltpu.VMEM((16, 4, 8, BLOCK), F32),
-            pltpu.VMEM((16, 4, 8, BLOCK), F32),
+            pltpu.VMEM((16, 3, 8, BLOCK), F32),
+            pltpu.VMEM((16, 3, 8, BLOCK), F32),
             *[wire(n) for n in (3, 2, 1, 0)],
             *[wire(n) for n in (3, 2, 1, 0)],
             pltpu.VMEM((8, 4, 32, 128), WIRE),
             pltpu.VMEM((8, 4, 32, 128), WIRE),
             pltpu.VMEM((2, 4, 32, 128), F32),
-            pltpu.VMEM((8, 4, 8, BLOCK), F32),
+            pltpu.VMEM((8, 3, 8, BLOCK), F32),
             dma((5,)), dma((5,)), dma((5,)),
             dma((4, 4, 4)), dma((4, 4, 4)), dma((15,)), dma,
             dma((8,)), dma, dma((7,)), dma, dma((15,)), dma((4,)), dma((4,)), dma((4,)),

time: 88 us -> 84.8 us (0.964)
  Pallas kernels: 87 us -> 83.8 us
    pallas_call x1, Pallas kernels: 84.2 us -> 81.1 us  [panels(): pl.pallas_call(panel_kernel, out_shape=(jax.ShapeDtypeStruct((PANEL, PANE...]
where the time goes in v5:
time: 84.8 us; the launch traced here: 84.6 us
  Pallas kernels  83.8 us (99%)
    pallas_call x1, Pallas kernels, panels(): pl.pallas_call(panel_kernel, out_shape=(jax.ShapeDtypeStruct((PANEL, PANE...  81.1 us
    pallas_call x1, Pallas kernels, on_device(): pl.pallas_call(finish_kernel, out_shape=(jax.ShapeDtypeStruct((1, PANEL,...  2.79 us

profile of v5, /device:TPU:1, one launch (start us, length us, event | category | flops | bytes accessed | tf_op | source)
XLA Modules:
  0.0 84.6 jit_solution(11530724089533667639)
XLA Ops:
  0.6 81.1 %panels.1 = (f32[512,512]{1,0:T(8,128)}, bf16[512,512]{1,0:T(8,128)(2,1)}) custom-call(bf16[512,8192]{1,0:T(8,128)(2,1)} %feat.1, f32[512]{0:T(512)} %prior.1), custom_call_target="tpu_custom_call" | custom-call | flops 4294967296 | bytes 10485760 | tf_op jit(solution)/shard_map/panels/pallas_call | solution.py:422
  81.7 2.8 %product.1 = (f32[1,512,512]{2,1,0:T(8,128)}, f32[1,512,1,512]{3,2,1,0:T(1,128)}) custom-call(f32[512,512]{1,0:T(8,128)} %get-tuple-element.4.panel, bf16[512,512]{1,0:T(8,128)(2,1)} %get-tuple-element.5.other), custom_call_target="tpu_custom_call" | custom-call | tf_op jit(solution)/shard_map/product/pallas_call | solution.py:552

commit v6 on v5

--- a/solution.py
+++ b/solution.py
@@ -535,16 +535,30 @@
     )
 
 
-def finish_kernel(panel, other, panel_out, update_out, product, sem):
-    panel_copy = pltpu.make_async_copy(panel, panel_out.at[0], sem.at[0])
-    panel_copy.start()
-    product[...] = jnp.dot(
-        panel[...].astype(jnp.bfloat16), other[...], preferred_element_type=F32
-    ) * (1.0 / PANEL)
-    product_copy = pltpu.make_async_copy(product, update_out.at[0, :, 0, :], sem.at[1])
-    product_copy.start()
-    panel_copy.wait()
-    product_copy.wait()
+def finish_kernel(panel, other, panel_out, update_out, left, right, product, sem):
+    strips = [pl.ds(128 * i, 128) for i in range(4)]
+    load = pltpu.make_async_copy(other, right, sem.at[0])
+    load.start()
+    loads = [
+        pltpu.make_async_copy(panel.at[at], left.at[at], sem.at[1 + i]) for i, at in enumerate(strips)
+    ]
+    for copy in loads:
+        copy.start()
+    load.wait()
+    stores = []
+    for i, at in enumerate(strips):
+        loads[i].wait()
+        stores.append(pltpu.make_async_copy(left.at[at], panel_out.at[0, at], sem.at[5 + i]))
+        stores[-1].start()
+        product[at] = jnp.dot(
+            left[at].astype(jnp.bfloat16), right[...], preferred_element_type=F32
+        ) * (1.0 / PANEL)
+        stores.append(
+            pltpu.make_async_copy(product.at[at], update_out.at[0, at, 0, :], sem.at[9 + i])
+        )
+        stores[-1].start()
+    for copy in stores:
+        copy.wait()
 
 
 def on_device(features, prior):
@@ -555,9 +569,14 @@
             jax.ShapeDtypeStruct((1, PANEL, PANEL), F32),
             jax.ShapeDtypeStruct((1, PANEL, 1, PANEL), F32),
         ),
-        in_specs=[pl.BlockSpec(memory_space=pltpu.VMEM)] * 2,
+        in_specs=[pl.BlockSpec(memory_space=pl.ANY)] * 2,
         out_specs=(pl.BlockSpec(memory_space=pl.ANY),) * 2,
-        scratch_shapes=[pltpu.VMEM((PANEL, PANEL), F32), pltpu.SemaphoreType.DMA((2,))],
+        scratch_shapes=[
+            pltpu.VMEM((PANEL, PANEL), F32),
+            pltpu.VMEM((PANEL, PANEL), jnp.bfloat16),
+            pltpu.VMEM((PANEL, PANEL), F32),
+            pltpu.SemaphoreType.DMA((13,)),
+        ],
         name="product",
     )(panel, other)
 

time: 84.8 us -> 84.9 us (level)
  no operation moved by 1% of the time
where the time goes in v6:
time: 84.9 us; the launch traced here: 84.7 us
  Pallas kernels  83.9 us (99%)
    pallas_call x1, Pallas kernels, panels(): pl.pallas_call(panel_kernel, out_shape=(jax.ShapeDtypeStruct((PANEL, PANE...  81.1 us
    pallas_call x1, Pallas kernels, on_device(): pl.pallas_call(finish_kernel, out_shape=(jax.ShapeDtypeStruct((1, PANEL,...  2.87 us

profile of v6, /device:TPU:1, one launch (start us, length us, event | category | flops | bytes accessed | tf_op | source)
XLA Modules:
  0.0 84.7 jit_solution(12880782045354154716)
XLA Ops:
  0.6 81.1 %panels.1 = (f32[512,512]{1,0:T(8,128)}, bf16[512,512]{1,0:T(8,128)(2,1)}) custom-call(bf16[512,8192]{1,0:T(8,128)(2,1)} %feat.1, f32[512]{0:T(512)} %prior.1), custom_call_target="tpu_custom_call" | custom-call | flops 4294967296 | bytes 10485760 | tf_op jit(solution)/shard_map/panels/pallas_call | solution.py:422
  81.7 2.9 %product.1 = (f32[1,512,512]{2,1,0:T(8,128)}, f32[1,512,1,512]{3,2,1,0:T(1,128)}) custom-call(f32[512,512]{1,0:T(8,128)} %get-tuple-element.4.panel, bf16[512,512]{1,0:T(8,128)(2,1)} %get-tuple-element.5.other), custom_call_target="tpu_custom_call" | custom-call | tf_op jit(solution)/shard_map/product/pallas_call | solution.py:566
